TPU v7x, 32 devices: a whole 2x2x4 slice. The times are simulated.
32 devices in a mesh: shard: 32 (over z, y, x, core).
Axes of the slice: x: 2, y: 2, z: 4, core: 2. Of those that a mesh axis runs over, the one named last changes fastest.
Arguments:
- features: bfloat16 [163840, 400], P('shard'), may hold values from -6 to 6
- counts: int32 [32], P('shard'), may hold values from 1706 to 5120, as said below
- labelled: int32 [163840], P('shard'), may hold values from 0 to 1, as said below
- labels: int32 [163840], P('shard'), may hold values from 0 to 46
- w_branch: float32 [400, 512], P(None, 'shard'), may hold values from -0.625 to 0.625
- w_mid: float32 [2048, 512], P(None, 'shard'), may hold values from -0.125 to 0.125
- w_head: float32 [512, 47], replicated, may hold values from -0.25 to 0.25
- small_params: float32 [9775], replicated, as said below
- mom_branch: float32 [400, 512], P(None, 'shard'), may hold values from -16 to 16
- mom_mid: float32 [2048, 512], P(None, 'shard'), may hold values from -28 to 28
- mom_head: float32 [512, 47], replicated, may hold values from -3072 to 3072
- mom_small: float32 [9775], replicated, may hold values from -20 to 20
- avg_branch: float32 [400, 512], P(None, 'shard'), may hold values from -0.625 to 0.625
- avg_mid: float32 [2048, 512], P(None, 'shard'), may hold values from -0.125 to 0.125
- avg_head: float32 [512, 47], replicated, may hold values from -0.25 to 0.25
- avg_small: float32 [9775], replicated, may hold values from -3 to 3
Outputs:
- logits: float32 [163840, 47], P('shard')
- features_grad: float32 [163840, 400], P('shard')
- grad_branch: float32 [400, 512], P(None, 'shard')
- grad_mid: float32 [2048, 512], P(None, 'shard')
- grad_head: float32 [512, 47], replicated
- grad_small: float32 [9775], replicated
- new_mom_branch: float32 [400, 512], P(None, 'shard')
- new_mom_mid: float32 [2048, 512], P(None, 'shard')
- new_mom_head: float32 [512, 47], replicated
- new_mom_small: float32 [9775], replicated
- new_avg_branch: float32 [400, 512], P(None, 'shard')
- new_avg_mid: float32 [2048, 512], P(None, 'shard')
- new_avg_head: float32 [512, 47], replicated
- new_avg_small: float32 [9775], replicated
- new_branch: float32 [400, 512], P(None, 'shard')
- new_mid: float32 [2048, 512], P(None, 'shard')
- new_head: float32 [512, 47], replicated
- new_small: float32 [9775], replicated
Inputs may be any that keep to these rules, and one draw needn't show every extreme that they name: `counts`: filled slots of each device's bucket; some device's bucket is full in every draw. `labelled`: the first slot of every device's bucket is a training node. `small_params`: gains near one, shifts and class bias of both signs, slopes between 0.05 and 0.45.
All inputs are finite; a program needn't handle non-finite values.
Results may differ from a plain program's by a relative error of at most 0.0076.
Values may be sent and summed in bfloat16 or wider, within the bound.
A program may use at most 320 MiB of HBM per device.

v0:
```python
import math
import jax
import jax.numpy as jnp
from jax import lax
from jax.sharding import PartitionSpec as P

K = 4
F = 100
H = 512
C = 47
EPS = 1e-05
MOMENTUM = 0.9
DECAY = 0.9


def prelu_apply(values_in, slopes):
    return slopes * values_in + (1.0 - slopes) * jax.nn.softplus(values_in)


def prelu_slope_term(values_in):
    return values_in - jax.nn.softplus(values_in)


def prelu_input_factor(values_in, slopes):
    return slopes + (1.0 - slopes) * jax.nn.sigmoid(values_in)


def split_small(packed):
    width = K * H
    return (
        packed[:width],
        packed[width : 2 * width],
        packed[2 * width : 3 * width],
        packed[3 * width : 4 * width],
        packed[4 * width : 4 * width + H],
        packed[4 * width + H : 4 * width + 2 * H],
        packed[4 * width + 2 * H : 4 * width + 3 * H],
        packed[4 * width + 3 * H :],
    )


def nesterov(weight, gradient, momentum_old, average_old, step_rate):
    momentum_new = MOMENTUM * momentum_old + gradient
    weight_new = weight - step_rate * (gradient + MOMENTUM * momentum_new)
    average_new = DECAY * average_old + (1.0 - DECAY) * weight_new
    return (momentum_new, average_new, weight_new)


def moments(columns_in, bucket):
    masked = columns_in * bucket[:, None]
    totals, count_fill = lax.psum((jnp.sum(masked, axis=0), jnp.sum(bucket)), "shard")
    mean_col = totals / count_fill
    centered = columns_in - mean_col
    squares = lax.psum(jnp.sum(centered * centered * bucket[:, None], axis=0), "shard")
    variance = squares / count_fill
    return (mean_col, lax.rsqrt(variance + EPS), count_fill)


def local(
    features,
    counts,
    labelled,
    labels,
    w_branch,
    w_mid,
    w_head,
    small_params,
    mom_branch,
    mom_mid,
    mom_head,
    mom_small,
    avg_branch,
    avg_mid,
    avg_head,
    avg_small,
):
    node_rows = features.shape[0]
    nodes_all = node_rows * lax.axis_size("shard")
    gain1, shift1, slope1, slope2, gain2, shift2, slope3, head_bias = split_small(small_params)
    slot_index = lax.broadcasted_iota(jnp.int32, (node_rows,), 0)
    bucket = (slot_index < counts[0]).astype(jnp.float32)
    trained = bucket * labelled.astype(jnp.float32)
    branch_low = w_branch.astype(jnp.bfloat16)
    mid_low = w_mid.astype(jnp.bfloat16)
    head_low = w_head.astype(jnp.bfloat16)
    branch_full = lax.all_gather(branch_low, "shard", axis=1, tiled=True)
    feats_three = features.reshape(node_rows, K, F)
    branch_three = branch_full.reshape(K, F, H)
    branch_pre = jnp.einsum(
        "nkf,kfh->nkh", feats_three, branch_three, preferred_element_type=jnp.float32
    ).reshape(node_rows, K * H)
    mean1, inv1, count_fill = moments(branch_pre, bucket)
    branch_hat = (branch_pre - mean1) * inv1
    branch_norm = gain1 * branch_hat + shift1
    branch_act = prelu_apply(branch_norm, slope1)
    concat_low = prelu_apply(branch_act, slope2).astype(jnp.bfloat16)
    mid_full = lax.all_gather(mid_low, "shard", axis=1, tiled=True)
    mid_pre = jnp.dot(concat_low, mid_full, preferred_element_type=jnp.float32)
    mean2, inv2, unused_fill = moments(mid_pre, bucket)
    mid_hat = (mid_pre - mean2) * inv2
    mid_norm = gain2 * mid_hat + shift2
    hidden_low = prelu_apply(mid_norm, slope3).astype(jnp.bfloat16)
    scores = jnp.dot(hidden_low, head_low, preferred_element_type=jnp.float32) + head_bias
    log_total = jax.nn.logsumexp(scores, axis=1)
    prob_rows = jnp.exp(scores - log_total[:, None])
    one_hot = (labels[:, None] == lax.broadcasted_iota(jnp.int32, (1, C), 1)).astype(jnp.float32)
    logit_low = ((prob_rows - one_hot) * trained[:, None]).astype(jnp.bfloat16)
    head_part = jnp.dot(hidden_low.T, logit_low, preferred_element_type=jnp.float32)
    bias_part = jnp.sum(logit_low.astype(jnp.float32), axis=0)
    hidden_grad = jnp.dot(logit_low, head_low.T, preferred_element_type=jnp.float32)
    slope_out_part = jnp.sum(hidden_grad * prelu_slope_term(mid_norm), axis=0)
    mid_norm_grad = hidden_grad * prelu_input_factor(mid_norm, slope3)
    grad_head, grad_bias, grad_slope3, grad_gain2, grad_shift2 = lax.psum(
        (
            head_part,
            bias_part,
            slope_out_part,
            jnp.sum(mid_norm_grad * mid_hat * bucket[:, None], axis=0),
            jnp.sum(mid_norm_grad * bucket[:, None], axis=0),
        ),
        "shard",
    )
    mid_grad_low = (
        gain2
        * inv2
        * bucket[:, None]
        * (mid_norm_grad - (grad_shift2 + mid_hat * grad_gain2) / count_fill)
    ).astype(jnp.bfloat16)
    mid_part = jnp.dot(concat_low.T, mid_grad_low, preferred_element_type=jnp.float32)
    concat_grad = jnp.dot(mid_grad_low, mid_full.T, preferred_element_type=jnp.float32)
    slope_two_part = jnp.sum(concat_grad * prelu_slope_term(branch_act), axis=0)
    act_grad = concat_grad * prelu_input_factor(branch_act, slope2)
    slope_one_part = jnp.sum(act_grad * prelu_slope_term(branch_norm), axis=0)
    norm_grad = act_grad * prelu_input_factor(branch_norm, slope1)
    grad_slope1, grad_slope2, grad_gain1, grad_shift1 = lax.psum(
        (
            slope_one_part,
            slope_two_part,
            jnp.sum(norm_grad * branch_hat * bucket[:, None], axis=0),
            jnp.sum(norm_grad * bucket[:, None], axis=0),
        ),
        "shard",
    )
    branch_grad_low = (
        gain1
        * inv1
        * bucket[:, None]
        * (norm_grad - (grad_shift1 + branch_hat * grad_gain1) / count_fill)
    ).astype(jnp.bfloat16)
    branch_grad_three = branch_grad_low.reshape(node_rows, K, H)
    features_grad = jnp.einsum(
        "nkh,kfh->nkf", branch_grad_three, branch_three, preferred_element_type=jnp.float32
    ).reshape(node_rows, K * F)
    branch_part = jnp.einsum(
        "nkf,nkh->kfh", feats_three, branch_grad_three, preferred_element_type=jnp.float32
    ).reshape(K * F, H)
    grad_branch, grad_mid = (
        lax.psum_scatter(branch_part, "shard", scatter_dimension=1, tiled=True),
        lax.psum_scatter(mid_part, "shard", scatter_dimension=1, tiled=True),
    )
    grad_small = jnp.concatenate(
        [
            grad_gain1,
            grad_shift1,
            grad_slope1,
            grad_slope2,
            grad_gain2,
            grad_shift2,
            grad_slope3,
            grad_bias,
        ]
    )
    root = math.sqrt(nodes_all)
    mom_b, avg_b, new_b = nesterov(w_branch, grad_branch, mom_branch, avg_branch, 0.8 / root)
    mom_m, avg_m, new_m = nesterov(w_mid, grad_mid, mom_mid, avg_mid, 0.08 / root)
    mom_h, avg_h, new_h = nesterov(w_head, grad_head, mom_head, avg_head, 0.3 / root)
    mom_s, avg_s, new_s = nesterov(small_params, grad_small, mom_small, avg_small, 1.0 / root)
    logits = scores * bucket[:, None]
    return (
        logits,
        features_grad,
        grad_branch,
        grad_mid,
        grad_head,
        grad_small,
        mom_b,
        mom_m,
        mom_h,
        mom_s,
        avg_b,
        avg_m,
        avg_h,
        avg_s,
        new_b,
        new_m,
        new_h,
        new_s,
    )


def solution(mesh):
    in_specs = (
        P("shard", None),
        P("shard"),
        P("shard"),
        P("shard"),
        P(None, "shard"),
        P(None, "shard"),
        P(),
        P(),
        P(None, "shard"),
        P(None, "shard"),
        P(),
        P(),
        P(None, "shard"),
        P(None, "shard"),
        P(),
        P(),
    )
    out_specs = (
        P("shard", None),
        P("shard", None),
        P(None, "shard"),
        P(None, "shard"),
        P(),
        P(),
        P(None, "shard"),
        P(None, "shard"),
        P(),
        P(),
        P(None, "shard"),
        P(None, "shard"),
        P(),
        P(),
        P(None, "shard"),
        P(None, "shard"),
        P(),
        P(),
    )
    return jax.shard_map(local, mesh=mesh, in_specs=in_specs, out_specs=out_specs, check_vma=False)
```

profile of v0, /device:TPU:0, one launch (start us, length us, event | category | flops | bytes accessed | tf_op | source)
XLA Modules:
  0.0 917.9 jit_solution(16101625293680502912)
XLA Ops:
  11.6 44.7 %all_gather.6 = bf16[400,512]{0,1:T(8,128)(2,1)S(1)} all-gather(bf16[400,16]{0,1:T(8,128)(2,1)S(1)} %convert_element_type.40), channel_id=1, replica_groups=mesh['shard'=32] {'shard'}, dimensions={1}, use_global_device_ids=true | all-gather | bytes 422400 | tf_op jit(solution)/shard_map/all_gather | solution.py:86
  56.6 4.1 reshape.110
  60.7 18.7 %fusion.4 = (f32[4,512]{1,0:T(4,128)S(1)}, f32[4,512,5120]{2,1,0:T(8,128)}) fusion(f32[5120]{0:T(1024)S(1)} %fusion.8, bf16[4,100,512]{2,1,0:T(8,128)(2,1)S(1)} %reshape.109, bf16[5120,4,100]{0,2,1:T(8,128)(2,1)} %reshape.110), kind=kOutput, calls=%fused_computation.9 | convolution fusion | flops 2118121472 | bytes 46477312 | tf_op jit(solution)/shard_map/nkf,kfh->nkh/dot_general | solution.py:89
  79.4 37.1 %all-reduce.2 = (f32[2048]{0:T(1024)S(1)}, f32[]{:T(128)}) all-reduce(f32[2048]{0:T(1024)S(1)} %bitcast.70, f32[]{:T(128)} %fusion.9), channel_id=1, replica_groups=mesh['shard'=32] {'shard'}, use_global_device_ids=true, to_apply=%region_1.0 | all-reduce | flops 2049 | bytes 16392 | tf_op jit(solution)/shard_map/psum | solution.py:51
  117.2 16.8 %fusion.3 = f32[4,512]{1,0:T(4,128)S(1)} fusion(f32[4,512,5120]{2,1,0:T(8,128)} %get-tuple-element.129, f32[4,512]{1,0:T(4,128)S(1)} %sub.91, f32[5120]{0:T(1024)S(1)} %fusion.8), kind=kLoop, calls=%fused_computation.8 | loop fusion | flops 41940992 | bytes 41979904 | tf_op jit(solution)/shard_map/reduce_sum | solution.py:54
  134.0 42.2 %psum.103 = f32[2048]{0:T(1024)S(1)} all-reduce(f32[2048]{0:T(1024)S(1)} %bitcast.71), channel_id=1, replica_groups=mesh['shard'=32] {'shard'}, use_global_device_ids=true, to_apply=%region_5.0 | all-reduce | flops 2048 | bytes 16384 | tf_op jit(solution)/shard_map/psum | solution.py:54
  177.5 66.5 %add_convert_fusion = (bf16[5120,2048]{0,1:T(8,128)(2,1)}, f32[5120,2048]{0,1:T(8,128)}) fusion(f32[2048]{0:T(1024)S(1)} %get-tuple-element.121, f32[2048]{0:T(1024)S(1)} %get-tuple-element.127, f32[2048]{0:T(1024)S(1)} %get-tuple-element.122, f32[2048]{0:T(1024)S(1)} %get-tuple-element.125, f32[2048]{0:T(1024)S(1)} %get-tuple-element.124, ...), kind=kLoop, calls=%fused_computation.17 | loop fusion | flops 241172480 | bytes 104923136 | tf_op jit(solution)/shard_map/convert_element_type | solution.py:96
  243.9 20.0 %multiply_reduce_fusion.8 = (f32[512]{0:T(512)S(1)}, f32[5120,512]{1,0:T(8,128)}) fusion(f32[5120]{0:T(1024)S(1)} %fusion.8, bf16[5120,2048]{0,1:T(8,128)(2,1)} %get-tuple-element.108, bf16[2048,512]{0,1:T(8,128)(2,1)} %all-gather.2.cloned.1.call-done), kind=kOutput, calls=%fused_computation.29 | convolution fusion | flops 10742661120 | bytes 33576960 | tf_op jit(solution)/shard_map/dot_general | solution.py:98
  264.0 39.5 %psum.104 = f32[512]{0:T(512)S(1)} all-reduce(f32[512]{0:T(512)S(1)} %get-tuple-element.130), channel_id=1, replica_groups=mesh['shard'=32] {'shard'}, use_global_device_ids=true, to_apply=%region_7.8 | all-reduce | flops 512 | bytes 4096 | tf_op jit(solution)/shard_map/psum | solution.py:51
  304.2 5.6 multiply_reduce_fusion.7
  309.7 40.7 %psum.105 = f32[512]{0:T(512)S(1)} all-reduce(f32[512]{0:T(512)S(1)} %multiply_reduce_fusion.7), channel_id=1, replica_groups=mesh['shard'=32] {'shard'}, use_global_device_ids=true, to_apply=%region_9.10 | all-reduce | flops 512 | bytes 4096 | tf_op jit(solution)/shard_map/psum | solution.py:54
  351.1 10.0 %add_convert_fusion.1 = bf16[5120,512]{1,0:T(8,128)(2,1)S(1)} fusion(f32[5120,512]{1,0:T(8,128)} %get-tuple-element.131, f32[512]{0:T(512)S(1)} %get-tuple-element.115, f32[512]{0:T(512)S(1)} %get-tuple-element.118, f32[512]{0:T(512)S(1)} %get-tuple-element.117, f32[512]{0:T(512)S(1)} %broadcast_divide_fusion.1, f32[512]{0:T(512)S(1)} %get-tuple-element.119, ...), kind=kLoop, calls=%fused_computation.26 | loop fusion | flops 36700160 | bytes 15740928 | tf_op jit(solution)/shard_map/convert_element_type | solution.py:102
  366.5 16.2 %multiply_reduce_fusion.6 = (f32[512]{0:T(512)S(1)}, f32[512]{0:T(512)S(1)}, f32[512]{0:T(512)}, f32[5120,512]{1,0:T(8,128)}) fusion(f32[5120]{0:T(1024)S(1)} %fusion.8, f32[512]{0:T(512)S(1)} %get-tuple-element.118, f32[512]{0:T(512)S(1)} %get-tuple-element.117, f32[5120,512]{1,0:T(8,128)} %get-tuple-element.131, f32[512]{0:T(512)S(1)} %broadcast_divide_fusion.1, ...), kind=kOutput, calls=%fused_computation.24 | convolution fusion | flops 309352448 | bytes 21587968 | tf_op jit(solution)/shard_map/dot_general | solution.py:110
  382.8 39.8 %all-reduce.1 = (f32[512]{0:T(512)S(1)}, f32[512]{0:T(512)S(1)}) all-reduce(f32[512]{0:T(512)S(1)} %get-tuple-element.77, f32[512]{0:T(512)S(1)} %get-tuple-element.76), channel_id=1, replica_groups=mesh['shard'=32] {'shard'}, use_global_device_ids=true, to_apply=%region_15.16 | all-reduce | flops 1024 | bytes 8192 | tf_op jit(solution)/shard_map/psum | solution.py:113
  422.6 11.1 %multiply_convert_fusion.1 = bf16[5120,512]{1,0:T(8,128)(2,1)S(1)} fusion(f32[5120,512]{1,0:T(8,128)} %get-tuple-element.131, f32[]{:T(128)} %get-tuple-element.88, f32[512]{0:T(512)S(1)} %get-tuple-element.85, f32[512]{0:T(512)S(1)} %get-tuple-element.86, f32[512]{0:T(512)S(1)} %get-tuple-element.116, f32[512]{0:T(512)S(1)} %get-tuple-element.117, ...), kind=kLoop, calls=%fused_computation.22 | loop fusion | flops 44564480 | bytes 26253316 | tf_op jit(solution)/shard_map/convert_element_type | solution.py:128
  433.8 109.1 %multiply_reduce_fusion = (f32[2048]{0:T(1024)S(1)}, f32[2048]{0:T(1024)S(1)}, f32[2048]{0:T(1024)S(1)}, f32[2048]{0:T(1024)S(1)}, f32[5120,2048]{0,1:T(8,128)}) fusion(f32[5120,2048]{0,1:T(8,128)} %get-tuple-element.109, f32[2048]{0:T(1024)S(1)} %get-tuple-element.125, f32[2048]{0:T(1024)S(1)} %get-tuple-element.124, f32[2048]{0:T(1024)S(1)} %broadcast_divide_fusion, ...), kind=kOutput, calls=%fused_computation.10 | convolution fusion | flops 11146354688 | bytes 133287936 | tf_op jit(solution)/shard_map/dot_general | solution.py:130
  542.9 41.6 %all-reduce = (f32[2048]{0:T(1024)S(1)}, f32[2048]{0:T(1024)S(1)}, f32[2048]{0:T(1024)S(1)}, f32[2048]{0:T(1024)S(1)}, f32[512]{0:T(512)S(1)}, /*index=5*/f32[47]{0:T(128)S(1)}) all-reduce(f32[2048]{0:T(1024)S(1)} %get-tuple-element.110, f32[2048]{0:T(1024)S(1)} %get-tuple-element.111, ...), channel_id=1, replica_groups=mesh['shard'=32] {'shard'}, use_global_device_ids=true, to_apply=%region_19.20 | all-reduce | flops 8751 | bytes 70008 | tf_op jit(solution)/shard_map/psum | solution.py:135
  584.5 34.9 %multiply_convert_fusion = bf16[5120,2048]{0,1:T(8,128)(2,1)} fusion(f32[5120,2048]{0,1:T(8,128)} %get-tuple-element.112, f32[4,512,5120]{2,1,0:T(8,128)} %get-tuple-element.129, f32[]{:T(128)} %get-tuple-element.88, f32[2048]{0:T(1024)S(1)} %get-tuple-element.79, f32[2048]{0:T(1024)S(1)} %get-tuple-element.80, f32[5120]{0:T(1024)S(1)} %fusion.8, ...), kind=kLoop, calls=%fused_computation.12 | loop fusion | flops 94371840 | bytes 104919040 | tf_op jit(solution)/shard_map/convert_element_type | solution.py:149
  619.4 12.0 %convolution_bitcast_fusion.1 = f32[4,100,512]{2,1,0:T(8,128)S(1)} fusion(bf16[5120,4,512]{0,2,1:T(8,128)(2,1)} %bitcast.64, bf16[5120,4,100]{0,2,1:T(8,128)(2,1)} %reshape.110), kind=kOutput, calls=%fused_computation.33 | convolution fusion | flops 2097152000 | bytes 25886720 | tf_op jit(solution)/shard_map/nkf,nkh->kfh/dot_general | solution.py:154
  632.9 18.2 %fusion.13 = f32[2048,512]{0,1:T(8,128)} fusion(bf16[5120,2048]{0,1:T(8,128)(2,1)} %get-tuple-element.108, bf16[5120,512]{1,0:T(8,128)(2,1)} %copy-done), kind=kOutput, calls=%fused_computation.80 | convolution fusion | flops 10737418240 | bytes 30408704 | tf_op jit(solution)/shard_map/dot_general | solution.py:129
  651.2 12.0 %convolution_bitcast_fusion = f32[5120,4,100]{0,2,1:T(8,128)} fusion(bf16[5120,4,512]{0,2,1:T(8,128)(2,1)} %bitcast.65, bf16[4,100,512]{2,1,0:T(8,128)(2,1)S(1)} %copy-done.2), kind=kOutput, calls=%fused_computation.31 | convolution fusion | flops 2097152000 | bytes 29573120 | tf_op jit(solution)/shard_map/nkh,kfh->nkf/dot_general | solution.py:151
  663.3 9.4 %reshape.113 = f32[5120,400]{0,1:T(8,128)} reshape(f32[5120,4,100]{0,2,1:T(8,128)} %convolution_bitcast_fusion) | data formatting | bytes 16384000 | tf_op jit(solution)/shard_map/reshape | solution.py:153
  675.1 93.1 %reduce-scatter.7.cloned.1.call-done = f32[16,400]{1,0:T(8,128)} async-done(((f32[512,400]{1,0:T(8,128)}), f32[16,400]{1,0:T(8,128)}) %reduce-scatter.7.cloned.1.call-update) | async-done | bytes 25616
  769.7 138.3 %reduce-scatter.5.cloned.1.call-done = f32[2048,16]{0,1:T(8,128)} async-done(((f32[2048,512]{0,1:T(8,128)}), f32[2048,16]{0,1:T(8,128)}) %reduce-scatter.5.cloned.1.call-update) | async-done | bytes 131088 | tf_op jit(solution)/shard_map/reduce_scatter | solution.py:159
  (100 shorter events, 21.3 us)
Async XLA Ops:
  7.2 236.7 %all-gather.2.cloned.1.call-start = ((), (), s32[]{:S(2)}) async-start(), calls=%async_computation.2 | async-start | bytes 2162688 | tf_op jit(solution)/shard_map/all_gather | solution.py:97
  8.8 664.7 %all-reduce.5.cloned.1.call-start = ((), (), s32[]{:S(2)}) async-start(), calls=%async_computation.4 | async-start | bytes 196608 | tf_op jit(solution)/shard_map/psum | solution.py:113
  56.6 22.8 %copy-start.1 = (bf16[4,100,512]{2,1,0:T(8,128)(2,1)}, bf16[4,100,512]{2,1,0:T(8,128)(2,1)S(1)}, u32[]{:S(2)}) copy-start(bf16[4,100,512]{2,1,0:T(8,128)(2,1)S(1)} %reshape.109) | copy-start | bytes 1228804
  117.1 59.0 %copy-start.6 = (f32[9775]{0:T(1024)S(1)}, f32[9775]{0:T(1024)}, u32[]{:S(2)}) copy-start(f32[9775]{0:T(1024)} %param.23) | copy-start | bytes 117304
  117.1 60.3 %copy-start.20 = (s32[5120]{0:T(1024)S(1)}, s32[5120]{0:T(1024)}, u32[]{:S(2)}) copy-start(s32[5120]{0:T(1024)} %param.18) | copy-start | bytes 61444
  309.7 51.4 %copy-start.4 = (f32[512,47]{0,1:T(8,128)S(1)}, f32[512,47]{0,1:T(8,128)}, u32[]{:S(2)}) copy-start(f32[512,47]{0,1:T(8,128)} %param.22) | copy-start | bytes 288772
  351.1 11.9 %copy-start.19 = (s32[5120]{0:T(1024)S(1)}, s32[5120]{0:T(1024)}, u32[]{:S(2)}) copy-start(s32[5120]{0:T(1024)} %param.19) | copy-start | bytes 61444
  382.7 385.5 %reduce-scatter.7.cloned.1.call-start = ((), (), s32[]{:S(2)}) async-start(), calls=%async_computation.5 | async-start | bytes 1081344
  422.6 11.1 %copy-start.21 = (f32[512]{0:T(512)}, f32[512]{0:T(512)S(1)}, u32[]{:S(2)}) copy-start(f32[512]{0:T(512)S(1)} %get-tuple-element.86) | copy-start | bytes 6148
  422.6 11.1 %copy-start.23 = (f32[512]{0:T(512)}, f32[512]{0:T(512)S(1)}, u32[]{:S(2)}) copy-start(f32[512]{0:T(512)S(1)} %get-tuple-element.85) | copy-start | bytes 6148
  433.7 109.1 %copy-start = (bf16[5120,512]{1,0:T(8,128)(2,1)}, bf16[5120,512]{1,0:T(8,128)(2,1)S(1)}, u32[]{:S(2)}) copy-start(bf16[5120,512]{1,0:T(8,128)(2,1)S(1)} %multiply_convert_fusion.1) | copy-start | bytes 15728644
  433.8 109.1 %copy-start.25 = (f32[512]{0:T(512)S(1)}, f32[512]{0:T(512)}, u32[]{:S(2)}) copy-start(f32[512]{0:T(512)} %get-tuple-element.78) | copy-start | bytes 6148
  433.8 109.1 %copy-start.26 = (f32[47]{0:T(128)S(1)}, f32[47]{0:T(128)}, u32[]{:S(2)}) copy-start(f32[47]{0:T(128)} %get-tuple-element.103) | copy-start | bytes 568
  433.8 150.7 %copy-start.16 = (f32[2048]{0:T(1024)S(1)}, f32[2048]{0:T(1024)}, u32[]{:S(2)}) copy-start(f32[2048]{0:T(1024)} %get-tuple-element.123) | copy-start | bytes 24580
  632.9 18.3 %copy-start.2 = (bf16[4,100,512]{2,1,0:T(8,128)(2,1)S(1)}, bf16[4,100,512]{2,1,0:T(8,128)(2,1)}, u32[]{:S(2)}) copy-start(bf16[4,100,512]{2,1,0:T(8,128)(2,1)} %copy-done.1) | copy-start | bytes 1228804
  632.9 275.1 %reduce-scatter.5.cloned.1.call-start = ((), (), s32[]{:S(2)}) async-start(), calls=%async_computation.3 | async-start | bytes 4325376 | tf_op jit(solution)/shard_map/reduce_scatter | solution.py:159
  663.2 10.3 %copy-start.5 = (f32[512,47]{0,1:T(8,128)S(1)}, f32[512,47]{0,1:T(8,128)}, u32[]{:S(2)}) copy-start(f32[512,47]{0,1:T(8,128)} %param.22) | copy-start | bytes 288772
  663.2 105.1 %copy-start.10 = (f32[400,16]{0,1:T(8,128)S(1)}, f32[400,16]{0,1:T(8,128)}, u32[]{:S(2)}) copy-start(f32[400,16]{0,1:T(8,128)} %param.20) | copy-start | bytes 76804
  663.2 105.1 %copy-start.17 = (f32[400,16]{0,1:T(8,128)S(1)}, f32[400,16]{0,1:T(8,128)}, u32[]{:S(2)}) copy-start(f32[400,16]{0,1:T(8,128)} %param.28) | copy-start | bytes 76804
  663.2 105.0 %copy-start.18 = (f32[400,16]{0,1:T(8,128)S(1)}, f32[400,16]{0,1:T(8,128)}, u32[]{:S(2)}) copy-start(f32[400,16]{0,1:T(8,128)} %param.24) | copy-start | bytes 76804
  663.3 244.7 %copy-start.3 = (f32[2048,16]{0,1:T(8,128)S(1)}, f32[2048,16]{0,1:T(8,128)}, u32[]{:S(2)}) copy-start(f32[2048,16]{0,1:T(8,128)} %param.21) | copy-start | bytes 393220
  663.3 244.7 %copy-start.8 = (f32[2048,16]{0,1:T(8,128)S(1)}, f32[2048,16]{0,1:T(8,128)}, u32[]{:S(2)}) copy-start(f32[2048,16]{0,1:T(8,128)} %param.29) | copy-start | bytes 393220
  663.3 244.7 %copy-start.9 = (f32[2048,16]{0,1:T(8,128)S(1)}, f32[2048,16]{0,1:T(8,128)}, u32[]{:S(2)}) copy-start(f32[2048,16]{0,1:T(8,128)} %param.25) | copy-start | bytes 393220
  672.8 238.4 %copy-start.13 = (f32[9775]{0:T(1024)}, f32[9775]{0:T(1024)S(1)}, u32[]{:S(2)}) copy-start(f32[9775]{0:T(1024)S(1)} %constant_dynamic-update-slice_fusion) | copy-start | bytes 117304
  (7 other events, 68.6 us)
Sparse Core Ops, SparseCore 0:
  11.5 59.4 all-gather.1
  382.9 120.6 all-reduce.4
  633.0 135.2 reduce-scatter.6
  771.1 136.8 reduce-scatter.4
where the time goes:
time: 924 us; the launch traced here: 918 us
  blocking collectives  286 us (31%)
  waiting for transfers between devices  232 us (25%)
  matrix products  209 us (23%)
  other arithmetic  158 us (17%)
  local copies, waits for them, and re-layouts  17.7 us (2%)
  between operations  15.1 us (2%)
    reduce_scatter x1, waiting for transfers between devices, local(): lax.psum_scatter(mid_part, 'shard', scatter_dimension=1, tiled=True)  138 us
    dot_general x1, matrix products, local(): jnp.dot(mid_grad_low, mid_full.T, preferred_element_type=jnp.float32)  109 us
    unnamed x5, waiting for transfers between devices  93.2 us
    psum x2, blocking collectives, moments(): lax.psum(jnp.sum(centered * centered * bucket[:, None], axis=0), 'shard')  82.9 us
    psum x2, blocking collectives, moments(): lax.psum((jnp.sum(masked, axis=0), jnp.sum(bucket)), 'shard')  76.6 us
    convert_element_type x1, other arithmetic, local(): concat_low = prelu_apply(branch_act, slope2).astype(jnp.bfloat16)  66.5 us
    all_gather x1, blocking collectives, local(): branch_full = lax.all_gather(branch_low, 'shard', axis=1, tiled=True)  44.7 us
    psum x1, blocking collectives, local(): lax.psum((slope_one_part, slope_two_part, jnp.sum(norm_grad * branch_hat...  41.6 us
  transfers between devices with their start and end apart: 4, of which 2 were waited for; matrix products, arithmetic and copies ran while one was open for 35% of the time, Pallas kernels for 0%

commit v1 on v0

--- a/solution.py
+++ b/solution.py
@@ -51,7 +51,9 @@
     totals, count_fill = lax.psum((jnp.sum(masked, axis=0), jnp.sum(bucket)), "shard")
     mean_col = totals / count_fill
     centered = columns_in - mean_col
-    squares = lax.psum(jnp.sum(centered * centered * bucket[:, None], axis=0), "shard")
+    x = jnp.sum(centered * centered * bucket[:, None], axis=0)
+    blocks = lax.all_gather(x, "shard", axis=0, tiled=False)
+    squares = blocks.sum(axis=0)
     variance = squares / count_fill
     return (mean_col, lax.rsqrt(variance + EPS), count_fill)
 

time: 924 us -> 918 us (level)
    psum x2 -> x0, blocking collectives: 82.9 us -> none  [moments(): lax.psum(jnp.sum(centered * centered * bucket[:, None], axis=0), 'shard')]
    all_gather x0 -> x2, blocking collectives: none -> 81.7 us  [moments(): blocks = lax.all_gather(x, 'shard', axis=0, tiled=False)]
    reduce_sum x2 -> x4, other arithmetic: 22.4 us -> 22.6 us  [the longest x2 22.4 us: moments(): x = jnp.sum(centered * centered * bucket[:, None], axis=0)]
where the time goes in v1:
time: 918 us; the launch traced here: 912 us
  blocking collectives  280 us (31%)
  waiting for transfers between devices  231 us (25%)
  matrix products  209 us (23%)
  other arithmetic  159 us (17%)
  local copies, waits for them, and re-layouts  17.7 us (2%)
  between operations  15.1 us (2%)
    reduce_scatter x1, waiting for transfers between devices, local(): lax.psum_scatter(mid_part, 'shard', scatter_dimension=1, tiled=True)  138 us
    dot_general x1, matrix products, local(): jnp.dot(mid_grad_low, mid_full.T, preferred_element_type=jnp.float32)  109 us
    unnamed x5, waiting for transfers between devices  92.9 us
    all_gather x2, blocking collectives, moments(): blocks = lax.all_gather(x, 'shard', axis=0, tiled=False)  81.7 us
    psum x2, blocking collectives, moments(): lax.psum((jnp.sum(masked, axis=0), jnp.sum(bucket)), 'shard')  74.1 us
    convert_element_type x1, other arithmetic, local(): concat_low = prelu_apply(branch_act, slope2).astype(jnp.bfloat16)  66.6 us
    all_gather x1, blocking collectives, local(): branch_full = lax.all_gather(branch_low, 'shard', axis=1, tiled=True)  44.7 us
    psum x1, blocking collectives, local(): lax.psum((slope_one_part, slope_two_part, jnp.sum(norm_grad * branch_hat...  41.9 us
  transfers between devices with their start and end apart: 4, of which 2 were waited for; matrix products, arithmetic and copies ran while one was open for 35% of the time, Pallas kernels for 0%

profile of v1, /device:TPU:0, one launch (start us, length us, event | category | flops | bytes accessed | tf_op | source)
XLA Modules:
  0.0 912.2 jit_solution(3993722798665691370)
XLA Ops:
  11.6 44.7 %all_gather.18 = bf16[400,512]{0,1:T(8,128)(2,1)S(1)} all-gather(bf16[400,16]{0,1:T(8,128)(2,1)S(1)} %convert_element_type.40), channel_id=1, replica_groups=mesh['shard'=32] {'shard'}, dimensions={1}, use_global_device_ids=true | all-gather | bytes 422400 | tf_op jit(solution)/shard_map/all_gather | solution.py:88
  56.6 4.1 reshape.119
  60.7 18.7 %fusion.4 = (f32[4,512]{1,0:T(4,128)S(1)}, f32[4,512,5120]{2,1,0:T(8,128)}) fusion(f32[5120]{0:T(1024)S(1)} %fusion.8, bf16[4,100,512]{2,1,0:T(8,128)(2,1)S(1)} %reshape.118, bf16[5120,4,100]{0,2,1:T(8,128)(2,1)} %reshape.119), kind=kOutput, calls=%fused_computation.9 | convolution fusion | flops 2118121472 | bytes 46477312 | tf_op jit(solution)/shard_map/nkf,kfh->nkh/dot_general | solution.py:91
  79.4 37.1 %all-reduce.2 = (f32[2048]{0:T(1024)S(1)}, f32[]{:T(128)}) all-reduce(f32[2048]{0:T(1024)S(1)} %bitcast.68, f32[]{:T(128)} %fusion.9), channel_id=1, replica_groups=mesh['shard'=32] {'shard'}, use_global_device_ids=true, to_apply=%region_1.0 | all-reduce | flops 2049 | bytes 16392 | tf_op jit(solution)/shard_map/psum | solution.py:51
  117.2 16.8 %fusion.3 = f32[4,512]{1,0:T(4,128)S(1)} fusion(f32[4,512,5120]{2,1,0:T(8,128)} %get-tuple-element.129, f32[4,512]{1,0:T(4,128)S(1)} %sub.91, f32[5120]{0:T(1024)S(1)} %fusion.8), kind=kLoop, calls=%fused_computation.8 | loop fusion | flops 41940992 | bytes 41979904 | tf_op jit(solution)/shard_map/reduce_sum | solution.py:54
  134.0 41.2 %all-gather.1 = f32[32,1,2048]{2,1,0:T(1,128)S(1)} all-gather(f32[1,1,2048]{2,1,0:T(1,128)S(1)} %reshape.125), channel_id=1, replica_groups=mesh['shard'=32] {'shard'}, dimensions={0}, use_global_device_ids=true | all-gather | bytes 270336 | tf_op jit(solution)/shard_map/all_gather | solution.py:55
  176.7 66.6 %add_convert_fusion = (bf16[5120,2048]{0,1:T(8,128)(2,1)}, f32[5120,2048]{0,1:T(8,128)}) fusion(f32[2048]{0:T(1024)S(1)} %get-tuple-element.121, f32[2048]{0:T(1024)S(1)} %get-tuple-element.127, f32[2048]{0:T(1024)S(1)} %get-tuple-element.122, f32[2048]{0:T(1024)S(1)} %get-tuple-element.125, f32[2048]{0:T(1024)S(1)} %get-tuple-element.124, ...), kind=kLoop, calls=%fused_computation.17 | loop fusion | flops 241172480 | bytes 104923136 | tf_op jit(solution)/shard_map/convert_element_type | solution.py:98
  243.3 19.9 %multiply_reduce_fusion.8 = (f32[512]{0:T(512)S(1)}, f32[5120,512]{1,0:T(8,128)}) fusion(f32[5120]{0:T(1024)S(1)} %fusion.8, bf16[5120,2048]{0,1:T(8,128)(2,1)} %get-tuple-element.108, bf16[2048,512]{0,1:T(8,128)(2,1)} %all-gather.5.cloned.1.call-done), kind=kOutput, calls=%fused_computation.29 | convolution fusion | flops 10742661120 | bytes 33576960 | tf_op jit(solution)/shard_map/dot_general | solution.py:100
  263.2 37.0 %psum.89 = f32[512]{0:T(512)S(1)} all-reduce(f32[512]{0:T(512)S(1)} %get-tuple-element.130), channel_id=1, replica_groups=mesh['shard'=32] {'shard'}, use_global_device_ids=true, to_apply=%region_7.8 | all-reduce | flops 512 | bytes 4096 | tf_op jit(solution)/shard_map/psum | solution.py:51
  300.9 5.6 multiply_reduce_fusion.7
  306.4 40.5 %all-gather.2 = f32[32,1,512]{2,1,0:T(1,128)S(1)} all-gather(f32[1,1,512]{2,1,0:T(1,128)S(1)} %bitcast.69), channel_id=2, replica_groups=mesh['shard'=32] {'shard'}, dimensions={0}, use_global_device_ids=true | all-gather | bytes 67584 | tf_op jit(solution)/shard_map/all_gather | solution.py:55
  347.7 10.0 %add_convert_fusion.1 = bf16[5120,512]{1,0:T(8,128)(2,1)S(1)} fusion(f32[5120,512]{1,0:T(8,128)} %get-tuple-element.131, f32[512]{0:T(512)S(1)} %get-tuple-element.115, f32[512]{0:T(512)S(1)} %get-tuple-element.118, f32[512]{0:T(512)S(1)} %get-tuple-element.117, f32[512]{0:T(512)S(1)} %broadcast_divide_fusion.1, f32[512]{0:T(512)S(1)} %get-tuple-element.119, ...), kind=kLoop, calls=%fused_computation.26 | loop fusion | flops 36700160 | bytes 15740928 | tf_op jit(solution)/shard_map/convert_element_type | solution.py:104
  363.1 16.2 %multiply_reduce_fusion.6 = (f32[512]{0:T(512)S(1)}, f32[512]{0:T(512)S(1)}, f32[512]{0:T(512)}, f32[5120,512]{1,0:T(8,128)}) fusion(f32[5120]{0:T(1024)S(1)} %fusion.8, f32[512]{0:T(512)S(1)} %get-tuple-element.118, f32[512]{0:T(512)S(1)} %get-tuple-element.117, f32[5120,512]{1,0:T(8,128)} %get-tuple-element.131, f32[512]{0:T(512)S(1)} %broadcast_divide_fusion.1, ...), kind=kOutput, calls=%fused_computation.24 | convolution fusion | flops 309352448 | bytes 21587968 | tf_op jit(solution)/shard_map/dot_general | solution.py:112
  379.4 37.4 %all-reduce.1 = (f32[512]{0:T(512)S(1)}, f32[512]{0:T(512)S(1)}) all-reduce(f32[512]{0:T(512)S(1)} %get-tuple-element.77, f32[512]{0:T(512)S(1)} %get-tuple-element.76), channel_id=1, replica_groups=mesh['shard'=32] {'shard'}, use_global_device_ids=true, to_apply=%region_15.16 | all-reduce | flops 1024 | bytes 8192 | tf_op jit(solution)/shard_map/psum | solution.py:115
  416.8 11.1 %multiply_convert_fusion.1 = bf16[5120,512]{1,0:T(8,128)(2,1)S(1)} fusion(f32[5120,512]{1,0:T(8,128)} %get-tuple-element.131, f32[]{:T(128)} %get-tuple-element.88, f32[512]{0:T(512)S(1)} %get-tuple-element.85, f32[512]{0:T(512)S(1)} %get-tuple-element.86, f32[512]{0:T(512)S(1)} %get-tuple-element.116, f32[512]{0:T(512)S(1)} %get-tuple-element.117, ...), kind=kLoop, calls=%fused_computation.22 | loop fusion | flops 44564480 | bytes 26253316 | tf_op jit(solution)/shard_map/convert_element_type | solution.py:130
  428.0 109.1 %multiply_reduce_fusion = (f32[2048]{0:T(1024)S(1)}, f32[2048]{0:T(1024)S(1)}, f32[2048]{0:T(1024)S(1)}, f32[2048]{0:T(1024)S(1)}, f32[5120,2048]{0,1:T(8,128)}) fusion(f32[5120,2048]{0,1:T(8,128)} %get-tuple-element.109, f32[2048]{0:T(1024)S(1)} %get-tuple-element.125, f32[2048]{0:T(1024)S(1)} %get-tuple-element.124, f32[2048]{0:T(1024)S(1)} %broadcast_divide_fusion, ...), kind=kOutput, calls=%fused_computation.10 | convolution fusion | flops 11146354688 | bytes 133287936 | tf_op jit(solution)/shard_map/dot_general | solution.py:132
  537.1 41.9 %all-reduce = (f32[2048]{0:T(1024)S(1)}, f32[2048]{0:T(1024)S(1)}, f32[2048]{0:T(1024)S(1)}, f32[2048]{0:T(1024)S(1)}, f32[512]{0:T(512)S(1)}, /*index=5*/f32[47]{0:T(128)S(1)}) all-reduce(f32[2048]{0:T(1024)S(1)} %get-tuple-element.110, f32[2048]{0:T(1024)S(1)} %get-tuple-element.111, ...), channel_id=1, replica_groups=mesh['shard'=32] {'shard'}, use_global_device_ids=true, to_apply=%region_19.20 | all-reduce | flops 8751 | bytes 70008 | tf_op jit(solution)/shard_map/psum | solution.py:137
  578.9 34.9 %multiply_convert_fusion = bf16[5120,2048]{0,1:T(8,128)(2,1)} fusion(f32[5120,2048]{0,1:T(8,128)} %get-tuple-element.112, f32[4,512,5120]{2,1,0:T(8,128)} %get-tuple-element.129, f32[]{:T(128)} %get-tuple-element.88, f32[2048]{0:T(1024)S(1)} %get-tuple-element.79, f32[2048]{0:T(1024)S(1)} %get-tuple-element.80, f32[5120]{0:T(1024)S(1)} %fusion.8, ...), kind=kLoop, calls=%fused_computation.12 | loop fusion | flops 94371840 | bytes 104919040 | tf_op jit(solution)/shard_map/convert_element_type | solution.py:151
  613.9 12.0 %convolution_bitcast_fusion.1 = f32[4,100,512]{2,1,0:T(8,128)S(1)} fusion(bf16[5120,4,512]{0,2,1:T(8,128)(2,1)} %bitcast.63, bf16[5120,4,100]{0,2,1:T(8,128)(2,1)} %reshape.119), kind=kOutput, calls=%fused_computation.33 | convolution fusion | flops 2097152000 | bytes 25886720 | tf_op jit(solution)/shard_map/nkf,nkh->kfh/dot_general | solution.py:156
  627.4 18.2 %fusion.13 = f32[2048,512]{0,1:T(8,128)} fusion(bf16[5120,2048]{0,1:T(8,128)(2,1)} %get-tuple-element.108, bf16[5120,512]{1,0:T(8,128)(2,1)} %copy-done), kind=kOutput, calls=%fused_computation.80 | convolution fusion | flops 10737418240 | bytes 30408704 | tf_op jit(solution)/shard_map/dot_general | solution.py:131
  645.7 12.0 %convolution_bitcast_fusion = f32[5120,4,100]{0,2,1:T(8,128)} fusion(bf16[5120,4,512]{0,2,1:T(8,128)(2,1)} %bitcast.64, bf16[4,100,512]{2,1,0:T(8,128)(2,1)S(1)} %copy-done.2), kind=kOutput, calls=%fused_computation.31 | convolution fusion | flops 2097152000 | bytes 29573120 | tf_op jit(solution)/shard_map/nkh,kfh->nkf/dot_general | solution.py:153
  657.8 9.4 %reshape.122 = f32[5120,400]{0,1:T(8,128)} reshape(f32[5120,4,100]{0,2,1:T(8,128)} %convolution_bitcast_fusion) | data formatting | bytes 16384000 | tf_op jit(solution)/shard_map/reshape | solution.py:155
  669.6 92.8 %reduce-scatter.7.cloned.1.call-done = f32[16,400]{1,0:T(8,128)} async-done(((f32[512,400]{1,0:T(8,128)}), f32[16,400]{1,0:T(8,128)}) %reduce-scatter.7.cloned.1.call-update) | async-done | bytes 25616
  763.9 138.3 %reduce-scatter.5.cloned.1.call-done = f32[2048,16]{0,1:T(8,128)} async-done(((f32[2048,512]{0,1:T(8,128)}), f32[2048,16]{0,1:T(8,128)}) %reduce-scatter.5.cloned.1.call-update) | async-done | bytes 131088 | tf_op jit(solution)/shard_map/reduce_scatter | solution.py:161
  (102 shorter events, 21.5 us)
Async XLA Ops:
  7.2 236.1 %all-gather.5.cloned.1.call-start = ((), (), s32[]{:S(2)}) async-start(), calls=%async_computation.2 | async-start | bytes 2162688 | tf_op jit(solution)/shard_map/all_gather | solution.py:99
  8.8 659.2 %all-reduce.5.cloned.1.call-start = ((), (), s32[]{:S(2)}) async-start(), calls=%async_computation.4 | async-start | bytes 196608 | tf_op jit(solution)/shard_map/psum | solution.py:115
  56.6 22.8 %copy-start.1 = (bf16[4,100,512]{2,1,0:T(8,128)(2,1)}, bf16[4,100,512]{2,1,0:T(8,128)(2,1)S(1)}, u32[]{:S(2)}) copy-start(bf16[4,100,512]{2,1,0:T(8,128)(2,1)S(1)} %reshape.118) | copy-start | bytes 1228804
  117.1 58.3 %copy-start.6 = (f32[9775]{0:T(1024)S(1)}, f32[9775]{0:T(1024)}, u32[]{:S(2)}) copy-start(f32[9775]{0:T(1024)} %param.23) | copy-start | bytes 117304
  117.1 59.5 %copy-start.20 = (s32[5120]{0:T(1024)S(1)}, s32[5120]{0:T(1024)}, u32[]{:S(2)}) copy-start(s32[5120]{0:T(1024)} %param.18) | copy-start | bytes 61444
  306.4 51.3 %copy-start.4 = (f32[512,47]{0,1:T(8,128)S(1)}, f32[512,47]{0,1:T(8,128)}, u32[]{:S(2)}) copy-start(f32[512,47]{0,1:T(8,128)} %param.22) | copy-start | bytes 288772
  347.7 11.9 %copy-start.19 = (s32[5120]{0:T(1024)S(1)}, s32[5120]{0:T(1024)}, u32[]{:S(2)}) copy-start(s32[5120]{0:T(1024)} %param.19) | copy-start | bytes 61444
  379.3 383.2 %reduce-scatter.7.cloned.1.call-start = ((), (), s32[]{:S(2)}) async-start(), calls=%async_computation.5 | async-start | bytes 1081344
  416.8 11.1 %copy-start.21 = (f32[512]{0:T(512)}, f32[512]{0:T(512)S(1)}, u32[]{:S(2)}) copy-start(f32[512]{0:T(512)S(1)} %get-tuple-element.86) | copy-start | bytes 6148
  416.8 11.1 %copy-start.23 = (f32[512]{0:T(512)}, f32[512]{0:T(512)S(1)}, u32[]{:S(2)}) copy-start(f32[512]{0:T(512)S(1)} %get-tuple-element.85) | copy-start | bytes 6148
  427.9 109.1 %copy-start = (bf16[5120,512]{1,0:T(8,128)(2,1)}, bf16[5120,512]{1,0:T(8,128)(2,1)S(1)}, u32[]{:S(2)}) copy-start(bf16[5120,512]{1,0:T(8,128)(2,1)S(1)} %multiply_convert_fusion.1) | copy-start | bytes 15728644
  427.9 109.1 %copy-start.25 = (f32[512]{0:T(512)S(1)}, f32[512]{0:T(512)}, u32[]{:S(2)}) copy-start(f32[512]{0:T(512)} %get-tuple-element.78) | copy-start | bytes 6148
  427.9 109.1 %copy-start.26 = (f32[47]{0:T(128)S(1)}, f32[47]{0:T(128)}, u32[]{:S(2)}) copy-start(f32[47]{0:T(128)} %get-tuple-element.103) | copy-start | bytes 568
  428.0 151.0 %copy-start.16 = (f32[2048]{0:T(1024)S(1)}, f32[2048]{0:T(1024)}, u32[]{:S(2)}) copy-start(f32[2048]{0:T(1024)} %get-tuple-element.123) | copy-start | bytes 24580
  627.3 18.3 %copy-start.2 = (bf16[4,100,512]{2,1,0:T(8,128)(2,1)S(1)}, bf16[4,100,512]{2,1,0:T(8,128)(2,1)}, u32[]{:S(2)}) copy-start(bf16[4,100,512]{2,1,0:T(8,128)(2,1)} %copy-done.1) | copy-start | bytes 1228804
  627.4 274.8 %reduce-scatter.5.cloned.1.call-start = ((), (), s32[]{:S(2)}) async-start(), calls=%async_computation.3 | async-start | bytes 4325376 | tf_op jit(solution)/shard_map/reduce_scatter | solution.py:161
  657.7 10.3 %copy-start.5 = (f32[512,47]{0,1:T(8,128)S(1)}, f32[512,47]{0,1:T(8,128)}, u32[]{:S(2)}) copy-start(f32[512,47]{0,1:T(8,128)} %param.22) | copy-start | bytes 288772
  657.7 104.7 %copy-start.10 = (f32[400,16]{0,1:T(8,128)S(1)}, f32[400,16]{0,1:T(8,128)}, u32[]{:S(2)}) copy-start(f32[400,16]{0,1:T(8,128)} %param.20) | copy-start | bytes 76804
  657.7 104.7 %copy-start.17 = (f32[400,16]{0,1:T(8,128)S(1)}, f32[400,16]{0,1:T(8,128)}, u32[]{:S(2)}) copy-start(f32[400,16]{0,1:T(8,128)} %param.28) | copy-start | bytes 76804
  657.8 104.7 %copy-start.18 = (f32[400,16]{0,1:T(8,128)S(1)}, f32[400,16]{0,1:T(8,128)}, u32[]{:S(2)}) copy-start(f32[400,16]{0,1:T(8,128)} %param.24) | copy-start | bytes 76804
  657.8 244.4 %copy-start.3 = (f32[2048,16]{0,1:T(8,128)S(1)}, f32[2048,16]{0,1:T(8,128)}, u32[]{:S(2)}) copy-start(f32[2048,16]{0,1:T(8,128)} %param.21) | copy-start | bytes 393220
  657.8 244.4 %copy-start.8 = (f32[2048,16]{0,1:T(8,128)S(1)}, f32[2048,16]{0,1:T(8,128)}, u32[]{:S(2)}) copy-start(f32[2048,16]{0,1:T(8,128)} %param.29) | copy-start | bytes 393220
  657.8 244.4 %copy-start.9 = (f32[2048,16]{0,1:T(8,128)S(1)}, f32[2048,16]{0,1:T(8,128)}, u32[]{:S(2)}) copy-start(f32[2048,16]{0,1:T(8,128)} %param.25) | copy-start | bytes 393220
  667.3 238.1 %copy-start.13 = (f32[9775]{0:T(1024)}, f32[9775]{0:T(1024)S(1)}, u32[]{:S(2)}) copy-start(f32[9775]{0:T(1024)S(1)} %constant_dynamic-update-slice_fusion) | copy-start | bytes 117304
  (7 other events, 68.6 us)
Sparse Core Ops, SparseCore 0:
  11.5 59.4 all-gather.4
  379.4 116.7 all-reduce.4
  627.5 134.9 reduce-scatter.6
  765.3 136.8 reduce-scatter.4
